TPU v7x, 32 devices: a whole 2x2x4 slice. The times are simulated.
32 devices in a mesh: head: 4 (over x, core), ctx: 2 (over y), inner: 4 (over z).
Axes of the slice: x: 2, y: 2, z: 4, core: 2. Of those that a mesh axis runs over, the one named last changes fastest.
Arguments:
- query_rows: bfloat16 [4096, 48, 128], P(('head', 'ctx', 'inner')), may hold values from -6 to 6
- key_rows: bfloat16 [4096, 48, 128], P(('head', 'ctx', 'inner')), may hold values from -6 to 6
- value_rows: bfloat16 [4096, 48, 128], P(('head', 'ctx', 'inner')), may hold values from -6 to 6
- grad_rows: bfloat16 [4096, 48, 128], P(('head', 'ctx', 'inner')), may hold values from -6 to 6
Outputs:
- grad_query: bfloat16 [4096, 48, 128], P(('head', 'ctx', 'inner'))
- grad_key: bfloat16 [4096, 48, 128], P(('head', 'ctx', 'inner'))
- grad_value: bfloat16 [4096, 48, 128], P(('head', 'ctx', 'inner'))
All inputs are finite; a program needn't handle non-finite values.
Results may differ from a plain program's by a relative error of at most 0.012.
The roundings to bfloat16 on the way count: a program that leaves them out, or rounds other values in their place, can miss the bound.
Values may be sent and summed in bfloat16 or wider, within the bound.
A program may use at most 128 MiB of HBM per device.

v0:
```python
import functools

import jax
import jax.numpy as jnp
from jax import lax
from jax.experimental import pallas as pl
from jax.experimental.pallas import tpu as pltpu
from jax.sharding import PartitionSpec as P

MESH = pl.DeviceIdType.MESH
BF16 = jnp.bfloat16
F32 = jnp.float32
CHUNK = 3
LAG = 1
LOW = -1e30


def dot_nt(a, b):
    return lax.dot_general(a, b, (((1,), (1,)), ((), ())), preferred_element_type=F32)


def dot_nn(a, b):
    return lax.dot_general(a, b, (((1,), (0,)), ((), ())), preferred_element_type=F32)


def dot_tn(a, b):
    return lax.dot_general(a, b, (((0,), (0,)), ((), ())), preferred_element_type=F32)


def kernel(
    sizes, x, out, own, prev, acc, partial, arrived, staged,
    kv_send, kv_recv, own_send, own_recv, own_local, grad_send, grad_recv,
    query_send, query_recv, query_local, result_send, result_recv, result_local,
):
    shards, inner = sizes
    heads, rows, width = x.shape[1:]
    mine = heads // 2
    chunks = mine // CHUNK
    scale = width ** -0.5
    log2_scale = scale * 1.4426950408889634

    head_at = lax.axis_index("head")
    shard = lax.axis_index("ctx") * inner + lax.axis_index("inner")
    half = head_at % 2
    other = 1 - half
    block = jnp.where(head_at < 2, shard, 2 * shards - 1 - shard)
    has_prev = block > 0
    has_next = block < 2 * shards - 1

    def device(at, side):
        low = at < shards
        to = jnp.where(low, at, 2 * shards - 1 - at)
        return (jnp.where(low, side, 2 + side), to // inner, to % inner)

    peer = device(block, other)
    after = jnp.where(has_next, block + 1, block - 1)
    before = jnp.where(has_prev, block - 1, block + 1)
    my_rows = pl.ds(pl.multiple_of(half * rows, rows), rows)
    peer_rows = pl.ds(pl.multiple_of(other * rows, rows), rows)

    def kv_copy(c, side):
        return pltpu.make_async_remote_copy(
            x.at[pl.ds(0, 2), pl.ds(side * mine + c * CHUNK, CHUNK)],
            prev.at[:, pl.ds(c * CHUNK, CHUNK), my_rows],
            kv_send.at[side, c], kv_recv.at[half, c], device(after, side), MESH,
        )

    def kv_arrival(c, side):
        return pltpu.make_async_remote_copy(
            x.at[pl.ds(0, 2), pl.ds(c * CHUNK, CHUNK)],
            prev.at[:, pl.ds(c * CHUNK, CHUNK), pl.ds(side * rows, rows)],
            kv_send.at[side, c], kv_recv.at[side, c], device(before, side), MESH,
        )

    def own_copy(c):
        return pltpu.make_async_remote_copy(
            x.at[:, pl.ds(other * mine + c * CHUNK, CHUNK)],
            own.at[:, pl.ds(c * CHUNK, CHUNK), my_rows],
            own_send.at[c], own_recv.at[c], peer, MESH,
        )

    def own_arrival(c):
        return pltpu.make_async_remote_copy(
            x.at[:, pl.ds(other * mine + c * CHUNK, CHUNK)],
            own.at[:, pl.ds(c * CHUNK, CHUNK), peer_rows],
            own_send.at[c], own_recv.at[c], peer, MESH,
        )

    def own_keep(c):
        return pltpu.make_async_copy(
            x.at[:, pl.ds(half * mine + c * CHUNK, CHUNK)],
            own.at[:, pl.ds(c * CHUNK, CHUNK), my_rows],
            own_local.at[c],
        )

    def grad_copy(c, to):
        return pltpu.make_async_remote_copy(
            partial.at[:, pl.ds(c * CHUNK, CHUNK)],
            arrived.at[:, pl.ds(c * CHUNK, CHUNK)],
            grad_send.at[c], grad_recv.at[c], device(to, half), MESH,
        )

    def out_copies(c, first, count, send, recv, local):
        kinds = pl.ds(first, count)
        here = pl.ds(c * CHUNK, CHUNK)
        remote = pltpu.make_async_remote_copy(
            staged.at[kinds, here, peer_rows],
            out.at[kinds, pl.ds(half * mine + c * CHUNK, CHUNK)],
            send.at[c], recv.at[c], peer, MESH,
        )
        arrival = pltpu.make_async_remote_copy(
            staged.at[kinds, here, peer_rows],
            out.at[kinds, pl.ds(other * mine + c * CHUNK, CHUNK)],
            send.at[c], recv.at[c], peer, MESH,
        )
        keep = pltpu.make_async_copy(
            staged.at[kinds, here, my_rows],
            out.at[kinds, pl.ds(half * mine + c * CHUNK, CHUNK)],
            local.at[c],
        )
        return remote, arrival, keep

    def query_out(c):
        return out_copies(c, 0, 1, query_send, query_recv, query_local)

    def result_out(c):
        return out_copies(c, 1, 2, result_send, result_recv, result_local)

    barrier = pltpu.get_barrier_semaphore()
    pl.semaphore_signal(barrier, inc=1, device_id=peer, device_id_type=MESH)

    @pl.when(has_next)
    def _():
        for side in range(2):
            pl.semaphore_signal(barrier, inc=1, device_id=device(after, side), device_id_type=MESH)

    @pl.when(has_prev)
    def _():
        for side in range(2):
            pl.semaphore_signal(barrier, inc=1, device_id=device(before, side), device_id_type=MESH)

    pl.semaphore_wait(
        barrier, 1 + jnp.where(has_next, 2, 0) + jnp.where(has_prev, 2, 0)
    )

    @pl.loop(0, chunks)
    def _(c):
        @pl.when(has_next)
        def _():
            kv_copy(c, 0).start()
            kv_copy(c, 1).start()

        own_copy(c).start()
        own_keep(c).start()

    @pl.when(jnp.logical_not(has_prev))
    def _():
        @pl.loop(0, mine)
        def _(j):
            prev[0, j] = jnp.zeros((2 * rows, width), BF16)
            prev[1, j] = jnp.zeros((2 * rows, width), BF16)

    @pl.when(jnp.logical_not(has_next))
    def _():
        @pl.loop(0, mine)
        def _(j):
            arrived[0, j] = jnp.zeros((2 * rows, width), BF16)
            arrived[1, j] = jnp.zeros((2 * rows, width), BF16)

    row_at = lax.broadcasted_iota(jnp.int32, (2 * rows, 2 * rows), 0)
    column_at = lax.broadcasted_iota(jnp.int32, (2 * rows, 2 * rows), 1)
    sees_own = column_at <= row_at
    sees_prev = column_at > row_at + jnp.where(has_prev, 0, 2 * rows)

    def one_head(j):
        key_prev, value_prev = prev[0, j], prev[1, j]
        key, value, query, grad = own[0, j], own[1, j], own[2, j], own[3, j]
        score_prev = jnp.where(sees_prev, dot_nt(query, key_prev), LOW)
        score_own = jnp.where(sees_own, dot_nt(query, key), LOW)
        top = jnp.maximum(
            jnp.max(score_prev, axis=-1, keepdims=True), jnp.max(score_own, axis=-1, keepdims=True)
        )
        prob_prev = jnp.exp2((score_prev - top) * log2_scale)
        prob_own = jnp.exp2((score_own - top) * log2_scale)
        total = jnp.sum(prob_prev, axis=-1, keepdims=True) + jnp.sum(
            prob_own, axis=-1, keepdims=True
        )
        inverse = 1.0 / total
        prob_prev = prob_prev * inverse
        prob_own = prob_own * inverse
        prob_prev_b = prob_prev.astype(BF16)
        prob_own_b = prob_own.astype(BF16)
        dprob_prev = dot_nt(grad, value_prev)
        dprob_own = dot_nt(grad, value)
        delta = jnp.sum(prob_prev_b.astype(F32) * dprob_prev, axis=-1, keepdims=True) + jnp.sum(
            prob_own_b.astype(F32) * dprob_own, axis=-1, keepdims=True
        )
        dscore_prev = (prob_prev * (dprob_prev - delta)).astype(BF16)
        dscore_own = (prob_own * (dprob_own - delta)).astype(BF16)
        partial[0, j] = (dot_tn(dscore_prev, query) * scale).astype(BF16)
        partial[1, j] = dot_tn(prob_prev_b, grad).astype(BF16)
        staged[0, j] = (
            (dot_nn(dscore_prev, key_prev) + dot_nn(dscore_own, key)) * scale
        ).astype(BF16)
        acc[0, j] = dot_tn(dscore_own, query) * scale
        acc[1, j] = dot_tn(prob_own_b, grad)

    def finish(c):
        @pl.when(has_next)
        def _():
            grad_copy(c, after).wait_recv()

        for at in range(CHUNK):
            j = c * CHUNK + at
            staged[1, j] = (acc[0, j] + arrived[0, j].astype(F32)).astype(BF16)
            staged[2, j] = (acc[1, j] + arrived[1, j].astype(F32)).astype(BF16)
        remote, _, keep = result_out(c)
        remote.start()
        keep.start()

    @pl.loop(0, chunks)
    def _(c):
        own_arrival(c).wait_recv()
        own_keep(c).wait()

        @pl.when(has_prev)
        def _():
            kv_arrival(c, 0).wait_recv()
            kv_arrival(c, 1).wait_recv()

        for at in range(CHUNK):
            one_head(c * CHUNK + at)

        @pl.when(has_prev)
        def _():
            grad_copy(c, before).start()

        remote, _, keep = query_out(c)
        remote.start()
        keep.start()

        @pl.when(c >= LAG)
        def _():
            finish(c - LAG)

    @pl.loop(chunks - LAG, chunks)
    def _(c):
        finish(c)

    @pl.loop(0, chunks)
    def _(c):
        own_copy(c).wait_send()

        @pl.when(has_next)
        def _():
            kv_copy(c, 0).wait_send()
            kv_copy(c, 1).wait_send()

        @pl.when(has_prev)
        def _():
            grad_copy(c, before).wait_send()

        for copies in (query_out(c), result_out(c)):
            remote, arrival, keep = copies
            remote.wait_send()
            arrival.wait_recv()
            keep.wait()


def on_device(shards, inner, query_rows, key_rows, value_rows, grad_rows):
    rows, heads, width = query_rows.shape
    stacked = jnp.stack([key_rows, value_rows, query_rows, grad_rows]).transpose(0, 2, 1, 3)
    mine = heads // 2
    chunks = mine // CHUNK
    dma = pltpu.SemaphoreType.DMA
    result = pl.pallas_call(
        functools.partial(kernel, (shards, inner)),
        out_shape=jax.ShapeDtypeStruct((3, heads, rows, width), BF16),
        in_specs=[pl.BlockSpec(memory_space=pl.ANY)],
        out_specs=pl.BlockSpec(memory_space=pl.ANY),
        scratch_shapes=[
            pltpu.VMEM((4, mine, 2 * rows, width), BF16),
            pltpu.VMEM((2, mine, 2 * rows, width), BF16),
            pltpu.VMEM((2, mine, 2 * rows, width), F32),
            pltpu.VMEM((2, mine, 2 * rows, width), BF16),
            pltpu.VMEM((2, mine, 2 * rows, width), BF16),
            pltpu.VMEM((3, mine, 2 * rows, width), BF16),
            dma((2, chunks)), dma((2, chunks)),
            dma((chunks,)), dma((chunks,)), dma((chunks,)),
            dma((chunks,)), dma((chunks,)),
            dma((chunks,)), dma((chunks,)), dma((chunks,)),
            dma((chunks,)), dma((chunks,)), dma((chunks,)),
        ],
        compiler_params=pltpu.CompilerParams(
            collective_id=0, has_side_effects=True, vmem_limit_bytes=48 * 1024 * 1024
        ),
        cost_estimate=pl.CostEstimate(
            flops=20 * mine * 4 * rows * rows * width,
            bytes_accessed=14 * heads * rows * width,
            transcendentals=mine * 8 * rows * rows,
        ),
    )(stacked)
    result = result.transpose(0, 2, 1, 3)
    return (result[0], result[1], result[2])


def solution(mesh):
    assert mesh.shape["head"] == 4
    shards = mesh.shape["ctx"] * mesh.shape["inner"]
    spec = P(("head", "ctx", "inner"), None, None)
    return jax.shard_map(
        functools.partial(on_device, shards, mesh.shape["inner"]),
        mesh=mesh,
        in_specs=(spec,) * 4,
        out_specs=(spec,) * 3,
        check_vma=False,
    )
```

profile of v0, /device:TPU:7, one launch (start us, length us, event | category | flops | bytes accessed | tf_op | source)
XLA Modules:
  0.0 158.5 jit_solution(333813650191420409)
XLA Ops:
  0.6 0.0 copy-start
  0.6 0.0 copy-start.1
  0.7 2.9 %copy_bitcast_fusion = (bf16[1,128,48,128]{3,1,2,0:T(8,128)(2,1)S(1)}, bf16[1,128,48,128]{3,1,2,0:T(8,128)(2,1)S(1)}) fusion(bf16[128,48,128]{2,1,0:T(8,128)(2,1)} %param.7, bf16[128,48,128]{2,1,0:T(8,128)(2,1)} %param.4), kind=kLoop, calls=%fused_computation.4 | loop fusion | bytes 6291456 | tf_op jit(solution)/shard_map/stack | solution.py:272
  3.5 0.0 copy-done
  3.5 0.0 copy-done.1
  3.5 0.8 copy_bitcast_fusion.2
  4.4 3.2 %maximum_bitcast_fusion.x = bf16[4,48,128,128]{3,2,1,0:T(8,128)(2,1)} fusion(bf16[1,128,48,128]{3,1,2,0:T(8,128)(2,1)S(1)} %get-tuple-element.9, bf16[1,128,48,128]{3,1,2,0:T(8,128)(2,1)S(1)} %get-tuple-element.10, bf16[1,128,48,128]{3,1,2,0:T(8,128)(2,1)S(1)} %get-tuple-element.11, bf16[1,128,48,128]{3,1,2,0:T(8,128)(2,1)S(1)} %get-tuple-element.12), kind=kLoop, calls=%fused_computation | loop fusion | flops 9437184 | bytes 12582912 | tf_op jit(solution)/shard_map/transpose | solution.py:272
  7.5 143.5 %shard_map.67 = bf16[3,48,128,128]{3,2,1,0:T(8,128)(2,1)S(1)} custom-call(bf16[4,48,128,128]{3,2,1,0:T(8,128)(2,1)} %maximum_bitcast_fusion.x), custom_call_target="tpu_custom_call" | custom-call | flops 4026531840 | bytes 11010048 | tf_op jit(solution)/shard_map/pallas_call | solution.py:276
  151.1 1.0 slice_bitcast_fusion
  152.0 2.2 %copy.13 = bf16[128,48,128]{2,1,0:T(8,128)(2,1)} copy(bf16[128,48,128]{2,0,1:T(8,128)(2,1)S(1)} %get-tuple-element.6) | data formatting | bytes 3145728
  154.2 2.2 %copy.12 = bf16[128,48,128]{2,1,0:T(8,128)(2,1)} copy(bf16[128,48,128]{2,0,1:T(8,128)(2,1)S(1)} %get-tuple-element.7) | data formatting | bytes 3145728
  156.3 2.2 %copy.11 = bf16[128,48,128]{2,1,0:T(8,128)(2,1)} copy(bf16[128,48,128]{2,0,1:T(8,128)(2,1)S(1)} %get-tuple-element.8) | data formatting | bytes 3145728
Async XLA Ops:
  0.6 2.9 %copy-start = (bf16[128,48,128]{2,1,0:T(8,128)(2,1)S(1)}, bf16[128,48,128]{2,1,0:T(8,128)(2,1)}, u32[]{:S(2)}) copy-start(bf16[128,48,128]{2,1,0:T(8,128)(2,1)} %param.6) | copy-start | bytes 4718596
  0.6 2.9 %copy-start.1 = (bf16[128,48,128]{2,1,0:T(8,128)(2,1)S(1)}, bf16[128,48,128]{2,1,0:T(8,128)(2,1)}, u32[]{:S(2)}) copy-start(bf16[128,48,128]{2,1,0:T(8,128)(2,1)} %param.5) | copy-start | bytes 4718596
where the time goes:
time: 159 us; the launch traced here: 158 us
  Pallas kernels  144 us (91%)
  local copies, waits for them, and re-layouts  11.1 us (7%)
  other arithmetic  3.18 us (2%)
    pallas_call x1, Pallas kernels, on_device(): pl.pallas_call(functools.partial(kernel, (shards, inner)), out_shape=jax....  144 us
    unnamed x7, local copies, waits for them, and re-layouts  6.48 us
    another operation x2, local copies, waits for them, and re-layouts, on_device(): jnp.stack([key_rows, value_rows, query_rows, grad_rows])  3.68 us
    transpose x1, other arithmetic, on_device(): jnp.stack([key_rows, value_rows, query_rows, grad_rows])  3.18 us

commit v1 on v0

--- a/solution.py
+++ b/solution.py
@@ -10,8 +10,8 @@
 MESH = pl.DeviceIdType.MESH
 BF16 = jnp.bfloat16
 F32 = jnp.float32
-CHUNK = 3
-LAG = 1
+CHUNK = 2
+LAG = 4
 LOW = -1e30
 
 
@@ -28,11 +28,13 @@
 
 
 def kernel(
-    sizes, x, out, own, prev, acc, partial, arrived, staged,
+    sizes, x, out, own, prev, acc, partial, arrived, staged, relay_kv, relay_grad,
     kv_send, kv_recv, own_send, own_recv, own_local, grad_send, grad_recv,
     query_send, query_recv, query_local, result_send, result_recv, result_local,
+    relay_send, relay_recv,
 ):
-    shards, inner = sizes
+    ctx, inner = sizes
+    shards = ctx * inner
     heads, rows, width = x.shape[1:]
     mine = heads // 2
     chunks = mine // CHUNK
@@ -40,7 +42,9 @@
     log2_scale = scale * 1.4426950408889634
 
     head_at = lax.axis_index("head")
-    shard = lax.axis_index("ctx") * inner + lax.axis_index("inner")
+    ctx_at = lax.axis_index("ctx")
+    inner_at = lax.axis_index("inner")
+    shard = ctx_at * inner + inner_at
     half = head_at % 2
     other = 1 - half
     block = jnp.where(head_at < 2, shard, 2 * shards - 1 - shard)
@@ -55,6 +59,19 @@
     peer = device(block, other)
     after = jnp.where(has_next, block + 1, block - 1)
     before = jnp.where(has_prev, block - 1, block + 1)
+    relays = ctx > 1 and inner > 2
+    is_first = inner_at == 0
+    is_last = inner_at == inner - 1
+    low_head = head_at < 2
+    can_rise = ctx_at < ctx - 1
+    can_fall = ctx_at > 0
+    low_corner = jnp.logical_and(is_first, can_rise)
+    high_corner = jnp.logical_and(is_last, can_fall)
+    wraps_next = jnp.logical_and(has_next, jnp.where(low_head, jnp.logical_and(is_last, can_rise), jnp.logical_and(is_first, can_fall)))
+    wraps_prev = jnp.logical_and(has_prev, jnp.where(low_head, jnp.logical_and(is_first, can_fall), jnp.logical_and(is_last, can_rise)))
+    kv_relay = jnp.where(low_head, high_corner, low_corner)
+    grad_relay = jnp.where(low_head, low_corner, high_corner)
+    mirror = inner - 1 - inner_at
     my_rows = pl.ds(pl.multiple_of(half * rows, rows), rows)
     peer_rows = pl.ds(pl.multiple_of(other * rows, rows), rows)
 
@@ -63,6 +80,41 @@
             x.at[pl.ds(0, 2), pl.ds(side * mine + c * CHUNK, CHUNK)],
             prev.at[:, pl.ds(c * CHUNK, CHUNK), my_rows],
             kv_send.at[side, c], kv_recv.at[half, c], device(after, side), MESH,
+        )
+
+    def relay_at(c):
+        return pl.ds((c // 2) * CHUNK, CHUNK)
+
+    def kv_detour(c, side):
+        return pltpu.make_async_remote_copy(
+            x.at[pl.ds(0, 2), pl.ds(side * mine + c * CHUNK, CHUNK)],
+            relay_kv.at[side, :, relay_at(c)],
+            kv_send.at[side, c], relay_recv.at[side, c // 2],
+            (head_at, jnp.where(low_head, ctx_at + 1, ctx_at - 1), inner_at), MESH,
+        )
+
+    def kv_forward(c, side):
+        return pltpu.make_async_remote_copy(
+            relay_kv.at[side, :, relay_at(c)],
+            prev.at[:, pl.ds(c * CHUNK, CHUNK), my_rows],
+            relay_send.at[side, c // 2], kv_recv.at[half, c],
+            (head_at - half + side, ctx_at, mirror), MESH,
+        )
+
+    def grad_detour(c):
+        return pltpu.make_async_remote_copy(
+            partial.at[:, pl.ds(c * CHUNK, CHUNK)],
+            relay_grad.at[:, relay_at(c)],
+            grad_send.at[c], relay_recv.at[2, c // 2],
+            (head_at, jnp.where(low_head, ctx_at - 1, ctx_at + 1), inner_at), MESH,
+        )
+
+    def grad_forward(c):
+        return pltpu.make_async_remote_copy(
+            relay_grad.at[:, relay_at(c)],
+            arrived.at[:, pl.ds(c * CHUNK, CHUNK)],
+            relay_send.at[2, c // 2], grad_recv.at[c],
+            (head_at, ctx_at, mirror), MESH,
         )
 
     def kv_arrival(c, side):
@@ -139,16 +191,50 @@
         for side in range(2):
             pl.semaphore_signal(barrier, inc=1, device_id=device(before, side), device_id_type=MESH)
 
-    pl.semaphore_wait(
-        barrier, 1 + jnp.where(has_next, 2, 0) + jnp.where(has_prev, 2, 0)
-    )
+    greeted = 1 + jnp.where(has_next, 2, 0) + jnp.where(has_prev, 2, 0)
+    if relays:
+        corner = jnp.logical_or(is_first, is_last)
+        rises = jnp.logical_and(corner, can_rise)
+        falls = jnp.logical_and(corner, can_fall)
+
+        @pl.when(corner)
+        def _():
+            for side in range(2):
+                pl.semaphore_signal(
+                    barrier, inc=1, device_id=(head_at - half + side, ctx_at, mirror),
+                    device_id_type=MESH,
+                )
+
+        @pl.when(rises)
+        def _():
+            pl.semaphore_signal(
+                barrier, inc=1, device_id=(head_at, ctx_at + 1, inner_at), device_id_type=MESH
+            )
+
+        @pl.when(falls)
+        def _():
+            pl.semaphore_signal(
+                barrier, inc=1, device_id=(head_at, ctx_at - 1, inner_at), device_id_type=MESH
+            )
+
+        greeted = greeted + jnp.where(corner, 2, 0)
+        greeted = greeted + jnp.where(rises, 1, 0) + jnp.where(falls, 1, 0)
+    pl.semaphore_wait(barrier, greeted)
 
     @pl.loop(0, chunks)
     def _(c):
-        @pl.when(has_next)
+        detour = jnp.logical_and(wraps_next, c % 2 == 1) if relays else False
+
+        @pl.when(jnp.logical_and(has_next, jnp.logical_not(detour)))
         def _():
             kv_copy(c, 0).start()
             kv_copy(c, 1).start()
+
+        if relays:
+            @pl.when(detour)
+            def _():
+                kv_detour(c, 0).start()
+                kv_detour(c, 1).start()
 
         own_copy(c).start()
         own_keep(c).start()
@@ -217,6 +303,11 @@
         remote, _, keep = result_out(c)
         remote.start()
         keep.start()
+        if relays:
+            @pl.when(jnp.logical_and(grad_relay, c % 2 == 1))
+            def _():
+                grad_detour(c).wait_recv()
+                grad_forward(c).start()
 
     @pl.loop(0, chunks)
     def _(c):
@@ -231,9 +322,22 @@
         for at in range(CHUNK):
             one_head(c * CHUNK + at)
 
-        @pl.when(has_prev)
+        detour = jnp.logical_and(wraps_prev, c % 2 == 1) if relays else False
+
+        @pl.when(jnp.logical_and(has_prev, jnp.logical_not(detour)))
         def _():
             grad_copy(c, before).start()
+
+        if relays:
+            @pl.when(detour)
+            def _():
+                grad_detour(c).start()
+
+            @pl.when(jnp.logical_and(kv_relay, c % 2 == 0))
+            def _():
+                for side in range(2):
+                    kv_detour(c + 1, side).wait_recv()
+                    kv_forward(c + 1, side).start()
 
         remote, _, keep = query_out(c)
         remote.start()
@@ -259,6 +363,16 @@
         @pl.when(has_prev)
         def _():
             grad_copy(c, before).wait_send()
+
+        if relays:
+            @pl.when(jnp.logical_and(kv_relay, c % 2 == 1))
+            def _():
+                kv_forward(c, 0).wait_send()
+                kv_forward(c, 1).wait_send()
+
+            @pl.when(jnp.logical_and(grad_relay, c % 2 == 1))
+            def _():
+                grad_forward(c).wait_send()
 
         for copies in (query_out(c), result_out(c)):
             remote, arrival, keep = copies
@@ -267,14 +381,14 @@
             keep.wait()
 
 
-def on_device(shards, inner, query_rows, key_rows, value_rows, grad_rows):
+def on_device(ctx, inner, query_rows, key_rows, value_rows, grad_rows):
     rows, heads, width = query_rows.shape
     stacked = jnp.stack([key_rows, value_rows, query_rows, grad_rows]).transpose(0, 2, 1, 3)
     mine = heads // 2
     chunks = mine // CHUNK
     dma = pltpu.SemaphoreType.DMA
     result = pl.pallas_call(
-        functools.partial(kernel, (shards, inner)),
+        functools.partial(kernel, (ctx, inner)),
         out_shape=jax.ShapeDtypeStruct((3, heads, rows, width), BF16),
         in_specs=[pl.BlockSpec(memory_space=pl.ANY)],
         out_specs=pl.BlockSpec(memory_space=pl.ANY),
@@ -285,11 +399,14 @@
             pltpu.VMEM((2, mine, 2 * rows, width), BF16),
             pltpu.VMEM((2, mine, 2 * rows, width), BF16),
             pltpu.VMEM((3, mine, 2 * rows, width), BF16),
+            pltpu.VMEM((2, 2, mine // 2, rows, width), BF16),
+            pltpu.VMEM((2, mine // 2, 2 * rows, width), BF16),
             dma((2, chunks)), dma((2, chunks)),
             dma((chunks,)), dma((chunks,)), dma((chunks,)),
             dma((chunks,)), dma((chunks,)),
             dma((chunks,)), dma((chunks,)), dma((chunks,)),
             dma((chunks,)), dma((chunks,)), dma((chunks,)),
+            dma((3, chunks // 2)), dma((3, chunks // 2)),
         ],
         compiler_params=pltpu.CompilerParams(
             collective_id=0, has_side_effects=True, vmem_limit_bytes=48 * 1024 * 1024
@@ -306,10 +423,9 @@
 
 def solution(mesh):
     assert mesh.shape["head"] == 4
-    shards = mesh.shape["ctx"] * mesh.shape["inner"]
     spec = P(("head", "ctx", "inner"), None, None)
     return jax.shard_map(
-        functools.partial(on_device, shards, mesh.shape["inner"]),
+        functools.partial(on_device, mesh.shape["ctx"], mesh.shape["inner"]),
         mesh=mesh,
         in_specs=(spec,) * 4,
         out_specs=(spec,) * 3,

time: 159 us -> 143 us (0.90)
  Pallas kernels: 144 us -> 127 us
    pallas_call x1, Pallas kernels: 144 us -> 127 us  [on_device(): pl.pallas_call(functools.partial(kernel, (ctx, inner)), out_shape=jax.Sha...]
where the time goes in v1:
time: 143 us; the launch traced here: 142 us
  Pallas kernels  127 us (89%)
  local copies, waits for them, and re-layouts  11.1 us (8%)
  other arithmetic  3.18 us (2%)
    pallas_call x1, Pallas kernels, on_device(): pl.pallas_call(functools.partial(kernel, (ctx, inner)), out_shape=jax.Sha...  127 us
    unnamed x7, local copies, waits for them, and re-layouts  6.48 us
    another operation x2, local copies, waits for them, and re-layouts, on_device(): jnp.stack([key_rows, value_rows, query_rows, grad_rows])  3.68 us
    transpose x1, other arithmetic, on_device(): jnp.stack([key_rows, value_rows, query_rows, grad_rows])  3.18 us

profile of v1, /device:TPU:7, one launch (start us, length us, event | category | flops | bytes accessed | tf_op | source)
XLA Modules:
  0.0 142.4 jit_solution(613814324890224017)
XLA Ops:
  0.6 0.0 copy-start
  0.6 0.0 copy-start.1
  0.7 2.9 %copy_bitcast_fusion = (bf16[1,128,48,128]{3,1,2,0:T(8,128)(2,1)S(1)}, bf16[1,128,48,128]{3,1,2,0:T(8,128)(2,1)S(1)}) fusion(bf16[128,48,128]{2,1,0:T(8,128)(2,1)} %param.7, bf16[128,48,128]{2,1,0:T(8,128)(2,1)} %param.4), kind=kLoop, calls=%fused_computation.4 | loop fusion | bytes 6291456 | tf_op jit(solution)/shard_map/stack | solution.py:386
  3.5 0.0 copy-done
  3.5 0.0 copy-done.1
  3.5 0.8 copy_bitcast_fusion.2
  4.4 3.2 %maximum_bitcast_fusion.x = bf16[4,48,128,128]{3,2,1,0:T(8,128)(2,1)} fusion(bf16[1,128,48,128]{3,1,2,0:T(8,128)(2,1)S(1)} %get-tuple-element.9, bf16[1,128,48,128]{3,1,2,0:T(8,128)(2,1)S(1)} %get-tuple-element.10, bf16[1,128,48,128]{3,1,2,0:T(8,128)(2,1)S(1)} %get-tuple-element.11, bf16[1,128,48,128]{3,1,2,0:T(8,128)(2,1)S(1)} %get-tuple-element.12), kind=kLoop, calls=%fused_computation | loop fusion | flops 9437184 | bytes 12582912 | tf_op jit(solution)/shard_map/transpose | solution.py:386
  7.5 127.4 %shard_map.67 = bf16[3,48,128,128]{3,2,1,0:T(8,128)(2,1)S(1)} custom-call(bf16[4,48,128,128]{3,2,1,0:T(8,128)(2,1)} %maximum_bitcast_fusion.x), custom_call_target="tpu_custom_call" | custom-call | flops 4026531840 | bytes 11010048 | tf_op jit(solution)/shard_map/pallas_call | solution.py:390
  134.9 1.0 slice_bitcast_fusion
  135.9 2.2 %copy.13 = bf16[128,48,128]{2,1,0:T(8,128)(2,1)} copy(bf16[128,48,128]{2,0,1:T(8,128)(2,1)S(1)} %get-tuple-element.6) | data formatting | bytes 3145728
  138.1 2.2 %copy.12 = bf16[128,48,128]{2,1,0:T(8,128)(2,1)} copy(bf16[128,48,128]{2,0,1:T(8,128)(2,1)S(1)} %get-tuple-element.7) | data formatting | bytes 3145728
  140.2 2.2 %copy.11 = bf16[128,48,128]{2,1,0:T(8,128)(2,1)} copy(bf16[128,48,128]{2,0,1:T(8,128)(2,1)S(1)} %get-tuple-element.8) | data formatting | bytes 3145728
Async XLA Ops:
  0.6 2.9 %copy-start = (bf16[128,48,128]{2,1,0:T(8,128)(2,1)S(1)}, bf16[128,48,128]{2,1,0:T(8,128)(2,1)}, u32[]{:S(2)}) copy-start(bf16[128,48,128]{2,1,0:T(8,128)(2,1)} %param.6) | copy-start | bytes 4718596
  0.6 2.9 %copy-start.1 = (bf16[128,48,128]{2,1,0:T(8,128)(2,1)S(1)}, bf16[128,48,128]{2,1,0:T(8,128)(2,1)}, u32[]{:S(2)}) copy-start(bf16[128,48,128]{2,1,0:T(8,128)(2,1)} %param.5) | copy-start | bytes 4718596

commit v2 on v1

--- a/solution.py
+++ b/solution.py
@@ -11,7 +11,8 @@
 BF16 = jnp.bfloat16
 F32 = jnp.float32
 CHUNK = 2
-LAG = 4
+GRAD_LAG = 4
+TILE = 16
 LOW = -1e30
 
 
@@ -28,16 +29,17 @@
 
 
 def kernel(
-    sizes, x, out, own, prev, acc, partial, arrived, staged, relay_kv, relay_grad,
+    sizes, key_rows, value_rows, query_rows, grad_rows, out, raw, x, own, prev, acc, partial, arrived, staged, relay_kv, relay_grad,
     kv_send, kv_recv, own_send, own_recv, own_local, grad_send, grad_recv,
     query_send, query_recv, query_local, result_send, result_recv, result_local,
-    relay_send, relay_recv,
+    relay_send, relay_recv, raw_sem,
 ):
     ctx, inner = sizes
     shards = ctx * inner
     heads, rows, width = x.shape[1:]
     mine = heads // 2
     chunks = mine // CHUNK
+    group = TILE // 2 // CHUNK
     scale = width ** -0.5
     log2_scale = scale * 1.4426950408889634
 
@@ -50,6 +52,14 @@
     block = jnp.where(head_at < 2, shard, 2 * shards - 1 - shard)
     has_prev = block > 0
     has_next = block < 2 * shards - 1
+
+    inputs = (key_rows, value_rows, query_rows, grad_rows)
+
+    def load(kind):
+        return pltpu.make_async_copy(inputs[kind], raw.at[kind], raw_sem.at[kind])
+
+    def heads_of(side, c):
+        return pl.ds((c // group) * TILE + side * (TILE // 2) + (c % group) * CHUNK, CHUNK)
 
     def device(at, side):
         low = at < shards
@@ -77,7 +87,7 @@
 
     def kv_copy(c, side):
         return pltpu.make_async_remote_copy(
-            x.at[pl.ds(0, 2), pl.ds(side * mine + c * CHUNK, CHUNK)],
+            x.at[pl.ds(0, 2), heads_of(side, c)],
             prev.at[:, pl.ds(c * CHUNK, CHUNK), my_rows],
             kv_send.at[side, c], kv_recv.at[half, c], device(after, side), MESH,
         )
@@ -87,7 +97,7 @@
 
     def kv_detour(c, side):
         return pltpu.make_async_remote_copy(
-            x.at[pl.ds(0, 2), pl.ds(side * mine + c * CHUNK, CHUNK)],
+            x.at[pl.ds(0, 2), heads_of(side, c)],
             relay_kv.at[side, :, relay_at(c)],
             kv_send.at[side, c], relay_recv.at[side, c // 2],
             (head_at, jnp.where(low_head, ctx_at + 1, ctx_at - 1), inner_at), MESH,
@@ -119,28 +129,28 @@
 
     def kv_arrival(c, side):
         return pltpu.make_async_remote_copy(
-            x.at[pl.ds(0, 2), pl.ds(c * CHUNK, CHUNK)],
+            x.at[pl.ds(0, 2), heads_of(side, c)],
             prev.at[:, pl.ds(c * CHUNK, CHUNK), pl.ds(side * rows, rows)],
             kv_send.at[side, c], kv_recv.at[side, c], device(before, side), MESH,
         )
 
     def own_copy(c):
         return pltpu.make_async_remote_copy(
-            x.at[:, pl.ds(other * mine + c * CHUNK, CHUNK)],
+            x.at[:, heads_of(other, c)],
             own.at[:, pl.ds(c * CHUNK, CHUNK), my_rows],
             own_send.at[c], own_recv.at[c], peer, MESH,
         )
 
     def own_arrival(c):
         return pltpu.make_async_remote_copy(
-            x.at[:, pl.ds(other * mine + c * CHUNK, CHUNK)],
+            x.at[:, heads_of(other, c)],
             own.at[:, pl.ds(c * CHUNK, CHUNK), peer_rows],
             own_send.at[c], own_recv.at[c], peer, MESH,
         )
 
     def own_keep(c):
         return pltpu.make_async_copy(
-            x.at[:, pl.ds(half * mine + c * CHUNK, CHUNK)],
+            x.at[:, heads_of(half, c)],
             own.at[:, pl.ds(c * CHUNK, CHUNK), my_rows],
             own_local.at[c],
         )
@@ -157,17 +167,17 @@
         here = pl.ds(c * CHUNK, CHUNK)
         remote = pltpu.make_async_remote_copy(
             staged.at[kinds, here, peer_rows],
-            out.at[kinds, pl.ds(half * mine + c * CHUNK, CHUNK)],
+            out.at[kinds, heads_of(half, c)],
             send.at[c], recv.at[c], peer, MESH,
         )
         arrival = pltpu.make_async_remote_copy(
             staged.at[kinds, here, peer_rows],
-            out.at[kinds, pl.ds(other * mine + c * CHUNK, CHUNK)],
+            out.at[kinds, heads_of(other, c)],
             send.at[c], recv.at[c], peer, MESH,
         )
         keep = pltpu.make_async_copy(
             staged.at[kinds, here, my_rows],
-            out.at[kinds, pl.ds(half * mine + c * CHUNK, CHUNK)],
+            out.at[kinds, heads_of(half, c)],
             local.at[c],
         )
         return remote, arrival, keep
@@ -177,6 +187,9 @@
 
     def result_out(c):
         return out_copies(c, 1, 2, result_send, result_recv, result_local)
+
+    for kind in range(4):
+        load(kind).start()
 
     barrier = pltpu.get_barrier_semaphore()
     pl.semaphore_signal(barrier, inc=1, device_id=peer, device_id_type=MESH)
@@ -221,8 +234,7 @@
         greeted = greeted + jnp.where(rises, 1, 0) + jnp.where(falls, 1, 0)
     pl.semaphore_wait(barrier, greeted)
 
-    @pl.loop(0, chunks)
-    def _(c):
+    def send_kv(c):
         detour = jnp.logical_and(wraps_next, c % 2 == 1) if relays else False
 
         @pl.when(jnp.logical_and(has_next, jnp.logical_not(detour)))
@@ -236,8 +248,29 @@
                 kv_detour(c, 0).start()
                 kv_detour(c, 1).start()
 
-        own_copy(c).start()
-        own_keep(c).start()
+    def turn(kind, g):
+        here = pl.ds(pl.multiple_of(g * TILE, TILE), TILE)
+        x[kind, here] = jnp.swapaxes(raw[kind, :, here, :], 0, 1)
+
+    for kind in range(4):
+        load(kind).wait()
+
+    @pl.loop(0, heads // TILE)
+    def _(g):
+        turn(0, g)
+        turn(1, g)
+
+        @pl.loop(0, group)
+        def _(at):
+            send_kv(g * group + at)
+
+        turn(2, g)
+        turn(3, g)
+
+        @pl.loop(0, group)
+        def _(at):
+            own_copy(g * group + at).start()
+            own_keep(g * group + at).start()
 
     @pl.when(jnp.logical_not(has_prev))
     def _():
@@ -303,11 +336,12 @@
         remote, _, keep = result_out(c)
         remote.start()
         keep.start()
-        if relays:
-            @pl.when(jnp.logical_and(grad_relay, c % 2 == 1))
-            def _():
-                grad_detour(c).wait_recv()
-                grad_forward(c).start()
+
+    def forward_grad(c):
+        @pl.when(jnp.logical_and(grad_relay, c % 2 == 0))
+        def _():
+            grad_detour(c).wait_recv()
+            grad_forward(c).start()
 
     @pl.loop(0, chunks)
     def _(c):
@@ -322,7 +356,7 @@
         for at in range(CHUNK):
             one_head(c * CHUNK + at)
 
-        detour = jnp.logical_and(wraps_prev, c % 2 == 1) if relays else False
+        detour = jnp.logical_and(wraps_prev, c % 2 == 0) if relays else False
 
         @pl.when(jnp.logical_and(has_prev, jnp.logical_not(detour)))
         def _():
@@ -343,11 +377,17 @@
         remote.start()
         keep.start()
 
-        @pl.when(c >= LAG)
-        def _():
-            finish(c - LAG)
-
-    @pl.loop(chunks - LAG, chunks)
+        if relays:
+            @pl.when(c >= GRAD_LAG)
+            def _():
+                forward_grad(c - GRAD_LAG)
+
+    if relays:
+        @pl.loop(chunks - GRAD_LAG, chunks)
+        def _(c):
+            forward_grad(c)
+
+    @pl.loop(0, chunks)
     def _(c):
         finish(c)
 
@@ -370,7 +410,7 @@
                 kv_forward(c, 0).wait_send()
                 kv_forward(c, 1).wait_send()
 
-            @pl.when(jnp.logical_and(grad_relay, c % 2 == 1))
+            @pl.when(jnp.logical_and(grad_relay, c % 2 == 0))
             def _():
                 grad_forward(c).wait_send()
 
@@ -383,16 +423,17 @@
 
 def on_device(ctx, inner, query_rows, key_rows, value_rows, grad_rows):
     rows, heads, width = query_rows.shape
-    stacked = jnp.stack([key_rows, value_rows, query_rows, grad_rows]).transpose(0, 2, 1, 3)
     mine = heads // 2
     chunks = mine // CHUNK
     dma = pltpu.SemaphoreType.DMA
     result = pl.pallas_call(
         functools.partial(kernel, (ctx, inner)),
         out_shape=jax.ShapeDtypeStruct((3, heads, rows, width), BF16),
-        in_specs=[pl.BlockSpec(memory_space=pl.ANY)],
+        in_specs=[pl.BlockSpec(memory_space=pl.ANY)] * 4,
         out_specs=pl.BlockSpec(memory_space=pl.ANY),
         scratch_shapes=[
+            pltpu.VMEM((4, rows, heads, width), BF16),
+            pltpu.VMEM((4, heads, rows, width), BF16),
             pltpu.VMEM((4, mine, 2 * rows, width), BF16),
             pltpu.VMEM((2, mine, 2 * rows, width), BF16),
             pltpu.VMEM((2, mine, 2 * rows, width), F32),
@@ -406,17 +447,17 @@
             dma((chunks,)), dma((chunks,)),
             dma((chunks,)), dma((chunks,)), dma((chunks,)),
             dma((chunks,)), dma((chunks,)), dma((chunks,)),
-            dma((3, chunks // 2)), dma((3, chunks // 2)),
+            dma((3, chunks // 2)), dma((3, chunks // 2)), dma((4,)),
         ],
         compiler_params=pltpu.CompilerParams(
-            collective_id=0, has_side_effects=True, vmem_limit_bytes=48 * 1024 * 1024
+            collective_id=0, has_side_effects=True, vmem_limit_bytes=56 * 1024 * 1024
         ),
         cost_estimate=pl.CostEstimate(
             flops=20 * mine * 4 * rows * rows * width,
             bytes_accessed=14 * heads * rows * width,
             transcendentals=mine * 8 * rows * rows,
         ),
-    )(stacked)
+    )(key_rows, value_rows, query_rows, grad_rows)
     result = result.transpose(0, 2, 1, 3)
     return (result[0], result[1], result[2])
 

time: 143 us -> 134 us (0.937)
  Pallas kernels: 127 us -> 123 us
  other arithmetic: 3.18 us -> 0 us
    pallas_call x1, Pallas kernels: 127 us -> 123 us  [on_device(): pl.pallas_call(functools.partial(kernel, (ctx, inner)), out_shape=jax.Sha...]
    another operation x2 -> x0, local copies, waits for them, and re-layouts: 3.68 us -> none  [on_device(): jnp.stack([key_rows, value_rows, query_rows, grad_rows])]
    transpose x1 -> x0, other arithmetic: 3.18 us -> none  [on_device(): jnp.stack([key_rows, value_rows, query_rows, grad_rows])]
    squeeze x1, local copies, waits for them, and re-layouts: 0.95 us -> 3.31 us  [on_device(): return (result[0], result[1], result[2])]
    unnamed x7 -> x3, local copies, waits for them, and re-layouts: 6.48 us -> 6.47 us
where the time goes in v2:
time: 134 us
  Pallas kernels  123 us (92%)
  local copies, waits for them, and re-layouts  9.78 us (7%)
    pallas_call x1, Pallas kernels, on_device(): pl.pallas_call(functools.partial(kernel, (ctx, inner)), out_shape=jax.Sha...  123 us
    unnamed x3, local copies, waits for them, and re-layouts  6.47 us
    squeeze x1, local copies, waits for them, and re-layouts, on_device(): return (result[0], result[1], result[2])  3.31 us

profile of v2, /device:TPU:7, one launch (start us, length us, event | category | flops | bytes accessed | tf_op | source)
XLA Modules:
  0.0 133.7 jit_solution(8544260590463418421)
XLA Ops:
  0.6 123.3 %shard_map.67 = bf16[3,48,128,128]{3,2,1,0:T(8,128)(2,1)} custom-call(bf16[128,48,128]{2,1,0:T(8,128)(2,1)} %key_rows.1, bf16[128,48,128]{2,1,0:T(8,128)(2,1)} %value_rows.1, bf16[128,48,128]{2,1,0:T(8,128)(2,1)} %query_rows.1, bf16[128,48,128]{2,1,0:T(8,128)(2,1)} %grad_rows.1), custom_call_target="tpu_custom_call" | custom-call | flops 4026531840 | bytes 11010048 | tf_op jit(solution)/shard_map/pallas_call | solution.py:429
  123.9 3.3 %slice_bitcast_fusion = (bf16[128,48,128]{2,0,1:T(8,128)(2,1)S(1)}, bf16[128,48,128]{2,0,1:T(8,128)(2,1)S(1)}, bf16[128,48,128]{2,0,1:T(8,128)(2,1)S(1)}) fusion(bf16[3,128,48,128]{3,1,2,0:T(8,128)(2,1)} %bitcast.7), kind=kLoop, calls=%fused_computation | loop fusion | bytes 9437184 | tf_op jit(solution)/shard_map/squeeze | solution.py:462
  127.3 2.2 %copy.9 = bf16[128,48,128]{2,1,0:T(8,128)(2,1)} copy(bf16[128,48,128]{2,0,1:T(8,128)(2,1)S(1)} %get-tuple-element.6) | data formatting | bytes 3145728
  129.4 2.2 %copy.8 = bf16[128,48,128]{2,1,0:T(8,128)(2,1)} copy(bf16[128,48,128]{2,0,1:T(8,128)(2,1)S(1)} %get-tuple-element.7) | data formatting | bytes 3145728
  131.6 2.2 %copy.7 = bf16[128,48,128]{2,1,0:T(8,128)(2,1)} copy(bf16[128,48,128]{2,0,1:T(8,128)(2,1)S(1)} %get-tuple-element.8) | data formatting | bytes 3145728

commit v3 on v2

--- a/solution.py
+++ b/solution.py
@@ -29,10 +29,11 @@
 
 
 def kernel(
-    sizes, key_rows, value_rows, query_rows, grad_rows, out, raw, x, own, prev, acc, partial, arrived, staged, relay_kv, relay_grad,
+    sizes, key_rows, value_rows, query_rows, grad_rows, grad_query, grad_key, grad_value,
+    raw, x, out, own, prev, acc, partial, arrived, staged, relay_kv, relay_grad,
     kv_send, kv_recv, own_send, own_recv, own_local, grad_send, grad_recv,
     query_send, query_recv, query_local, result_send, result_recv, result_local,
-    relay_send, relay_recv, raw_sem,
+    relay_send, relay_recv, raw_sem, turned_sem,
 ):
     ctx, inner = sizes
     shards = ctx * inner
@@ -387,9 +388,58 @@
         def _(c):
             forward_grad(c)
 
-    @pl.loop(0, chunks)
-    def _(c):
-        finish(c)
+    outputs = (grad_query, grad_key, grad_value)
+
+    def turned(kind, g):
+        here = pl.ds(pl.multiple_of(g * TILE, TILE), TILE)
+        return pltpu.make_async_copy(
+            raw.at[kind, :, here], outputs[kind].at[:, here], turned_sem.at[kind, g]
+        )
+
+    def turn_back(kind, g):
+        here = pl.ds(pl.multiple_of(g * TILE, TILE), TILE)
+        raw[kind, :, here] = jnp.swapaxes(out[kind, here], 0, 1)
+        turned(kind, g).start()
+
+    def landed(copies):
+        _, arrival, keep = copies
+        arrival.wait_recv()
+        keep.wait()
+
+    def results_back(g):
+        @pl.loop(0, group)
+        def _(at):
+            landed(result_out(g * group + at))
+
+        turn_back(1, g)
+        turn_back(2, g)
+
+    groups = heads // TILE
+
+    @pl.loop(0, groups)
+    def _(g):
+        @pl.loop(0, group)
+        def _(at):
+            landed(query_out(g * group + at))
+
+        turn_back(0, g)
+
+    @pl.loop(0, groups)
+    def _(g):
+        @pl.loop(0, group)
+        def _(at):
+            finish(g * group + at)
+
+        @pl.when(g > 0)
+        def _():
+            results_back(g - 1)
+
+    results_back(groups - 1)
+
+    @pl.loop(0, groups)
+    def _(g):
+        for kind in range(3):
+            turned(kind, g).wait()
 
     @pl.loop(0, chunks)
     def _(c):
@@ -415,10 +465,7 @@
                 grad_forward(c).wait_send()
 
         for copies in (query_out(c), result_out(c)):
-            remote, arrival, keep = copies
-            remote.wait_send()
-            arrival.wait_recv()
-            keep.wait()
+            copies[0].wait_send()
 
 
 def on_device(ctx, inner, query_rows, key_rows, value_rows, grad_rows):
@@ -428,12 +475,13 @@
     dma = pltpu.SemaphoreType.DMA
     result = pl.pallas_call(
         functools.partial(kernel, (ctx, inner)),
-        out_shape=jax.ShapeDtypeStruct((3, heads, rows, width), BF16),
+        out_shape=[jax.ShapeDtypeStruct((rows, heads, width), BF16)] * 3,
         in_specs=[pl.BlockSpec(memory_space=pl.ANY)] * 4,
-        out_specs=pl.BlockSpec(memory_space=pl.ANY),
+        out_specs=[pl.BlockSpec(memory_space=pl.ANY)] * 3,
         scratch_shapes=[
             pltpu.VMEM((4, rows, heads, width), BF16),
             pltpu.VMEM((4, heads, rows, width), BF16),
+            pltpu.VMEM((3, heads, rows, width), BF16),
             pltpu.VMEM((4, mine, 2 * rows, width), BF16),
             pltpu.VMEM((2, mine, 2 * rows, width), BF16),
             pltpu.VMEM((2, mine, 2 * rows, width), F32),
@@ -447,7 +495,7 @@
             dma((chunks,)), dma((chunks,)),
             dma((chunks,)), dma((chunks,)), dma((chunks,)),
             dma((chunks,)), dma((chunks,)), dma((chunks,)),
-            dma((3, chunks // 2)), dma((3, chunks // 2)), dma((4,)),
+            dma((3, chunks // 2)), dma((3, chunks // 2)), dma((4,)), dma((3, heads // TILE)),
         ],
         compiler_params=pltpu.CompilerParams(
             collective_id=0, has_side_effects=True, vmem_limit_bytes=56 * 1024 * 1024
@@ -458,8 +506,7 @@
             transcendentals=mine * 8 * rows * rows,
         ),
     )(key_rows, value_rows, query_rows, grad_rows)
-    result = result.transpose(0, 2, 1, 3)
-    return (result[0], result[1], result[2])
+    return tuple(result)
 
 
 def solution(mesh):

time: 134 us -> 131 us (0.978)
  local copies, waits for them, and re-layouts: 9.78 us -> 5.89 us
    squeeze x1 -> x0, local copies, waits for them, and re-layouts: 3.31 us -> none  [on_device(): return (result[0], result[1], result[2])]
    unnamed x3 -> x7, local copies, waits for them, and re-layouts: 6.47 us -> 5.89 us
where the time goes in v3:
time: 131 us
  Pallas kernels  124 us (95%)
  local copies, waits for them, and re-layouts  5.89 us (4%)
    pallas_call x1, Pallas kernels, on_device(): pl.pallas_call(functools.partial(kernel, (ctx, inner)), out_shape=[jax.Sh...  124 us
    unnamed x7, local copies, waits for them, and re-layouts  5.89 us

profile of v3, /device:TPU:7, one launch (start us, length us, event | category | flops | bytes accessed | tf_op | source)
XLA Modules:
  0.0 130.8 jit_solution(15267132374398169993)
XLA Ops:
  0.6 124.2 %shard_map.67 = (bf16[128,48,128]{2,1,0:T(8,128)(2,1)}, bf16[128,48,128]{2,1,0:T(8,128)(2,1)}, bf16[128,48,128]{2,1,0:T(8,128)(2,1)}) custom-call(bf16[128,48,128]{2,1,0:T(8,128)(2,1)} %key_rows.1, bf16[128,48,128]{2,1,0:T(8,128)(2,1)} %value_rows.1, bf16[128,48,128]{2,1,0:T(8,128)(2,1)} %query_rows.1, bf16[128,48,128]{2,1,0:T(8,128)(2,1)} %grad_rows.1), custom_call_target="tpu_custom_call" | custom-call | flops 4026531840 | bytes 11010048 | tf_op jit(solution)/shard_map/pallas_call | solution.py:476
  124.9 0.0 copy-start.1
  124.9 2.8 %copy.10 = bf16[128,48,128]{2,1,0:T(8,128)(2,1)} copy(bf16[128,48,128]{2,1,0:T(8,128)(2,1)} %get-tuple-element.6) | data formatting | bytes 3145728
  127.6 0.0 copy-done.1
  127.6 0.0 copy-start
  127.6 1.1 copy.11
  128.8 0.8 copy-done
  129.6 1.1 copy.12
Async XLA Ops:
  124.9 2.8 %copy-start.1 = (bf16[128,48,128]{2,1,0:T(8,128)(2,1)S(1)}, bf16[128,48,128]{2,1,0:T(8,128)(2,1)}, u32[]{:S(2)}) copy-start(bf16[128,48,128]{2,1,0:T(8,128)(2,1)} %get-tuple-element.7) | copy-start | bytes 4718596
  127.6 2.0 %copy-start = (bf16[128,48,128]{2,1,0:T(8,128)(2,1)S(1)}, bf16[128,48,128]{2,1,0:T(8,128)(2,1)}, u32[]{:S(2)}) copy-start(bf16[128,48,128]{2,1,0:T(8,128)(2,1)} %get-tuple-element.8) | copy-start | bytes 4718596

commit v4 on v3

--- a/solution.py
+++ b/solution.py
@@ -13,6 +13,7 @@
 CHUNK = 2
 GRAD_LAG = 4
 TILE = 16
+PARTS = 4
 LOW = -1e30
 
 
@@ -466,6 +467,24 @@
 
         for copies in (query_out(c), result_out(c)):
             copies[0].wait_send()
+
+
+def hand_over(*refs):
+    kinds = len(refs) // 2
+    sem = refs[-1]
+    copies = []
+    for kind in range(kinds):
+        source, target = refs[kind], refs[kinds + kind]
+        count = source.shape[0] // PARTS
+        for part in range(PARTS):
+            here = pl.ds(part * count, count)
+            copies.append(
+                pltpu.make_async_copy(source.at[here], target.at[here], sem.at[kind, part])
+            )
+    for copy in copies:
+        copy.start()
+    for copy in copies:
+        copy.wait()
 
 
 def on_device(ctx, inner, query_rows, key_rows, value_rows, grad_rows):
@@ -506,7 +525,16 @@
             transcendentals=mine * 8 * rows * rows,
         ),
     )(key_rows, value_rows, query_rows, grad_rows)
-    return tuple(result)
+    kinds = len(result)
+    return tuple(
+        pl.pallas_call(
+            hand_over,
+            out_shape=[jax.ShapeDtypeStruct((rows, heads, width), BF16)] * kinds,
+            in_specs=[pl.BlockSpec(memory_space=pl.ANY)] * kinds,
+            out_specs=[pl.BlockSpec(memory_space=pl.ANY)] * kinds,
+            scratch_shapes=[dma((kinds, PARTS))],
+        )(*result)
+    )
 
 
 def solution(mesh):

time: 131 us -> 269 us (2.05)
  Pallas kernels: 124 us -> 268 us
  local copies, waits for them, and re-layouts: 5.89 us -> 0 us
    pallas_call x0 -> x1, Pallas kernels: none -> 144 us  [on_device(): pl.pallas_call(hand_over, out_shape=[jax.ShapeDtypeStruct((rows, heads, w...]
    unnamed x7 -> x0, local copies, waits for them, and re-layouts: 5.89 us -> none
where the time goes in v4:
time: 269 us
  Pallas kernels  268 us (100%)
    pallas_call x1, Pallas kernels, on_device(): pl.pallas_call(hand_over, out_shape=[jax.ShapeDtypeStruct((rows, heads, w...  144 us
    pallas_call x1, Pallas kernels, on_device(): pl.pallas_call(functools.partial(kernel, (ctx, inner)), out_shape=[jax.Sh...  124 us

profile of v4, /device:TPU:7, one launch (start us, length us, event | category | flops | bytes accessed | tf_op | source)
XLA Modules:
  0.0 269.0 jit_solution(4758325966710489334)
XLA Ops:
  0.6 124.2 %shard_map.67 = (bf16[128,48,128]{2,1,0:T(8,128)(2,1)}, bf16[128,48,128]{2,1,0:T(8,128)(2,1)}, bf16[128,48,128]{2,1,0:T(8,128)(2,1)}) custom-call(bf16[128,48,128]{2,1,0:T(8,128)(2,1)} %key_rows.1, bf16[128,48,128]{2,1,0:T(8,128)(2,1)} %value_rows.1, bf16[128,48,128]{2,1,0:T(8,128)(2,1)} %query_rows.1, bf16[128,48,128]{2,1,0:T(8,128)(2,1)} %grad_rows.1), custom_call_target="tpu_custom_call" | custom-call | flops 4026531840 | bytes 11010048 | tf_op jit(solution)/shard_map/pallas_call | solution.py:495
  124.9 144.2 %shard_map.68 = (bf16[128,48,128]{2,1,0:T(8,128)(2,1)}, bf16[128,48,128]{2,1,0:T(8,128)(2,1)}, bf16[128,48,128]{2,1,0:T(8,128)(2,1)}) custom-call(bf16[128,48,128]{2,1,0:T(8,128)(2,1)} %get-tuple-element.6.refs_0_, bf16[128,48,128]{2,1,0:T(8,128)(2,1)} %get-tuple-element.7.refs_1_, bf16[128,48,128]{2,1,0:T(8,128)(2,1)} %get-tuple-element.8.refs_2_), custom_call_target="tpu_custom_call" | custom-call | tf_op jit(solution)/shard_map/pallas_call | solution.py:530
